TPU v7x, 32 devices: a whole 2x2x4 slice. The times are simulated.
32 devices in a mesh: dp: 8 (over z, y), mp: 4 (over x, core).
Axes of the slice: x: 2, y: 2, z: 4, core: 2. Of those that a mesh axis runs over, the one named last changes fastest.
Arguments:
- inputs: bfloat16 [8, 512, 4096], P('dp', None, 'mp'), may hold values from -6 to 6
- out_grads: bfloat16 [8, 512, 4096], P('dp', None, 'mp'), may hold values from -6 to 6
- gate_weight: bfloat16 [4096, 14336], P('dp', 'mp'), may hold values from -0.09375 to 0.09375
- down_weight: bfloat16 [14336, 4096], P('mp', 'dp'), may hold values from -0.046875 to 0.046875
- in_proj: bfloat16 [4096, 64], replicated, may hold values from -0.09375 to 0.09375
- out_proj: bfloat16 [14336, 64], P('mp'), may hold values from -0.046875 to 0.046875
- in_precond: float32 [64, 64], replicated, may hold values from -0.75 to 0.75
- out_precond: float32 [64, 64], replicated, may hold values from -0.75 to 0.75
- queries: bfloat16 [1024, 4096], P('dp', 'mp'), may hold values from -48 to 48
- languages: int32 [1024], P('dp'), may hold values from 0 to 31, as said below
Outputs:
- influence: float32 [8, 32], P('dp')
Inputs may be any that keep to these rules, and one draw needn't show every extreme that they name: Each of the 32 languages labels exactly 32 queries.
All inputs are finite; a program needn't handle non-finite values.
Results may differ from a plain program's by a relative error of at most 0.0042.
Values may be sent and summed in bfloat16 or wider, within the bound.
A program may use at most 128 MiB of HBM per device.

v0:
```python
import jax
import jax.numpy as jnp
from jax import lax
from jax.sharding import PartitionSpec as P

LANGS = 32


def shards(
    inputs,
    out_grads,
    gate_weight,
    down_weight,
    in_proj,
    out_proj,
    in_precond,
    out_precond,
    queries,
    languages,
):
    examples = inputs.shape[0]
    seq_len = inputs.shape[1]
    rows_full, grads_full = (
        lax.all_gather(inputs, "mp", axis=2, tiled=True),
        lax.all_gather(out_grads, "mp", axis=2, tiled=True),
    )
    tok_rows = rows_full.reshape(examples * seq_len, rows_full.shape[2])
    tok_grads = grads_full.reshape(examples * seq_len, grads_full.shape[2])
    columns = tok_rows
    gate = jnp.dot(
        columns,
        lax.all_gather(gate_weight, "dp", axis=0, tiled=True),
        preferred_element_type=jnp.float32,
    )
    columns = tok_grads
    hidden_grad = lax.dot_general(
        columns,
        lax.all_gather(down_weight, "dp", axis=1, tiled=True),
        (((1,), (1,)), ((), ())),
        preferred_element_type=jnp.float32,
    )
    up_grad = (hidden_grad * jax.nn.silu(gate)).astype(jnp.bfloat16)
    rank = in_proj.shape[1]
    band = rank // lax.axis_size("mp")
    in_factor = jnp.dot(
        jnp.dot(tok_rows, in_proj, preferred_element_type=jnp.float32),
        in_precond.T,
        precision=lax.Precision.HIGHEST,
    )
    in_three = in_factor.reshape(examples, seq_len, rank)
    out_part = jnp.dot(up_grad, out_proj, preferred_element_type=jnp.float32)
    out_sum = lax.psum(out_part, "mp")
    out_factor = jnp.dot(out_sum, out_precond, precision=lax.Precision.HIGHEST)
    full = (
        jnp.einsum(
            "esi,esj->eij",
            in_three,
            out_factor.reshape(examples, seq_len, rank),
            precision=lax.Precision.HIGHEST,
        )
        / seq_len
    )
    own_block = lax.dynamic_slice_in_dim(full, lax.axis_index("mp") * band, band, 1)
    projected = own_block.reshape(examples, band * rank).astype(jnp.bfloat16)
    per_language = languages.shape[0] * lax.axis_size("dp") // LANGS
    lang_ids = jnp.arange(LANGS, dtype=jnp.int32)
    query_piece = lax.all_gather(queries, "dp", axis=0, tiled=True)
    label_piece = lax.all_gather(languages, "dp", axis=0, tiled=True)
    block_scores = lax.dot_general(
        projected, query_piece, (((1,), (1,)), ((), ())), preferred_element_type=jnp.float32
    )
    onehot = (label_piece[:, None] == lang_ids[None, :]).astype(jnp.float32)
    partial_sums = jnp.dot(block_scores, onehot, precision=lax.Precision.HIGHEST)
    totals = lax.psum(partial_sums, "mp")
    return totals / per_language


def solution(mesh):
    return jax.shard_map(
        shards,
        mesh=mesh,
        in_specs=(
            P("dp", None, "mp"),
            P("dp", None, "mp"),
            P("dp", "mp"),
            P("mp", "dp"),
            P(),
            P("mp", None),
            P(),
            P(),
            P("dp", "mp"),
            P("dp"),
        ),
        out_specs=P("dp", None),
        check_vma=False,
    )
```

profile of v0, /device:TPU:0, one launch (start us, length us, event | category | flops | bytes accessed | tf_op | source)
XLA Modules:
  0.0 1330.7 jit_solution(5980809920941628300)
XLA Ops:
  6.5 0.0 copy-start
  6.5 0.0 all-gather.7.cloned.1.call-start
  6.5 0.7 all-gather.7.cloned.1.call-update
  7.3 0.0 all-gather.13.cloned.1.call-start
  7.3 0.7 all-gather.13.cloned.1.call-update
  8.0 0.0 all-gather.9.cloned.1.call-start
  8.1 0.7 all-gather.9.cloned.1.call-update
  8.7 0.0 all-gather.11.cloned.1.call-start
  8.8 0.5 all-gather.11.cloned.1.call-update
  9.3 0.0 all-reduce.2.cloned.1.call-start
  9.4 36.8 %all-gather.7.cloned.1.call-done = bf16[1,512,4096]{2,1,0:T(8,128)(2,1)} async-done(((bf16[1,512,1024]{2,1,0:T(8,128)(2,1)}), bf16[1,512,4096]{2,1,0:T(8,128)(2,1)}) %all-gather.7.cloned.1.call-update) | async-done | bytes 4194320 | tf_op jit(solution)/shard_map/all_gather | solution.py:24
  46.1 560.7 %all-gather.13.cloned.1.call-done = bf16[4096,3584]{1,0:T(8,128)(2,1)} async-done(((bf16[512,3584]{1,0:T(8,128)(2,1)}), bf16[4096,3584]{1,0:T(8,128)(2,1)}) %all-gather.13.cloned.1.call-update) | async-done | bytes 29360144 | tf_op jit(solution)/shard_map/all_gather | solution.py:32
  606.8 23.7 %fusion.1 = f32[512,3584]{1,0:T(8,128)} fusion(bf16[4096,3584]{1,0:T(8,128)(2,1)} %all-gather.13.cloned.1.call-done, bf16[1,512,4096]{2,1,0:T(8,128)(2,1)} %all-gather.7.cloned.1.call-done), kind=kOutput, calls=%fused_computation.2 | convolution fusion | flops 15032385536 | bytes 40894464 | tf_op jit(solution)/shard_map/dot_general | solution.py:30
  630.5 0.0 copy-start.4
  630.5 12.3 all-gather.9.cloned.1.call-done
  642.8 560.5 %all-gather.11.cloned.1.call-done = bf16[3584,4096]{1,0:T(8,128)(2,1)} async-done(((bf16[3584,512]{1,0:T(8,128)(2,1)}), bf16[3584,4096]{1,0:T(8,128)(2,1)}) %all-gather.11.cloned.1.call-update) | async-done | bytes 29360144 | tf_op jit(solution)/shard_map/all_gather | solution.py:38
  1203.4 24.2 %multiply_convert_fusion = bf16[512,3584]{1,0:T(8,128)(2,1)} fusion(f32[512,3584]{1,0:T(8,128)} %fusion.1, bf16[3584,4096]{1,0:T(8,128)(2,1)} %all-gather.11.cloned.1.call-done, bf16[1,512,4096]{2,1,0:T(8,128)(2,1)} %all-gather.9.cloned.1.call-done), kind=kOutput, calls=%fused_computation | convolution fusion | flops 15043395584 | bytes 44564480 | tf_op jit(solution)/shard_map/dot_general | solution.py:36
  1227.6 0.0 copy-done.4
  1227.6 0.0 copy-start.3
  1227.6 0.0 copy-start.1
  1227.6 3.8 fusion.9
  1231.4 0.0 copy-start.2
  1231.4 0.0 all-reduce.2.cloned.1.call-update
  1231.4 0.0 all-gather.15.cloned.1.call-start
  1231.5 0.5 all-gather.15.cloned.1.call-update
  1232.0 0.0 copy-done.3
  1232.0 19.4 %all-gather = s32[8,1,128]{2,1,0:T(1,128)S(1)} all-gather(s32[1,1,128]{2,1,0:T(1,128)S(1)} %bitcast.29), channel_id=1, replica_groups=mesh['dp'=8,'mp'=4] {'dp'}, dimensions={0}, use_global_device_ids=true | all-gather | bytes 4608 | tf_op jit(solution)/shard_map/all_gather | solution.py:68
  1251.4 0.0 copy-done
  1251.4 3.5 fusion.3
  1254.9 0.0 copy-done.1
  1254.9 0.4 fusion.8
  1255.3 8.3 all-reduce.2.cloned.1.call-done
  1263.5 0.0 copy-done.2
  1263.5 1.3 fusion.10
  1264.9 0.6 fusion.11
  1265.5 0.1 reshape.32
  1265.6 49.5 %all-gather.15.cloned.1.call-done = bf16[1024,1024]{1,0:T(8,128)(2,1)} async-done(((bf16[128,1024]{1,0:T(8,128)(2,1)}), bf16[1024,1024]{1,0:T(8,128)(2,1)}) %all-gather.15.cloned.1.call-update) | async-done | bytes 2097168 | tf_op jit(solution)/shard_map/all_gather | solution.py:67
  1315.1 2.2 convolution_bitcast_fusion
  1317.3 0.4 fusion.5
  1317.7 5.7 psum.15
  1323.4 0.5 broadcast_multiply_fusion
  (1 shorter events, 0.0 us)
Async XLA Ops:
  6.5 1244.9 %copy-start = (bf16[4096,64]{0,1:T(8,128)(2,1)S(1)}, bf16[4096,64]{0,1:T(8,128)(2,1)}, u32[]{:S(2)}) copy-start(bf16[4096,64]{0,1:T(8,128)(2,1)} %param.14) | copy-start | bytes 1572868
  6.5 39.6 %all-gather.7.cloned.1.call-start = ((), (), s32[]{:S(2)}) async-start(), calls=%async_computation | async-start | bytes 5242880 | tf_op jit(solution)/shard_map/all_gather | solution.py:24
  7.3 599.5 %all-gather.13.cloned.1.call-start = ((), (), s32[]{:S(2)}) async-start(), calls=%async_computation.3 | async-start | bytes 33030144 | tf_op jit(solution)/shard_map/all_gather | solution.py:32
  8.0 634.8 %all-gather.9.cloned.1.call-start = ((), (), s32[]{:S(2)}) async-start(), calls=%async_computation.1 | async-start | bytes 5242880 | tf_op jit(solution)/shard_map/all_gather | solution.py:25
  8.7 1194.6 %all-gather.11.cloned.1.call-start = ((), (), s32[]{:S(2)}) async-start(), calls=%async_computation.2 | async-start | bytes 33030144 | tf_op jit(solution)/shard_map/all_gather | solution.py:38
  9.3 1254.2 %all-reduce.2.cloned.1.call-start = ((), (), s32[]{:S(2)}) async-start(), calls=%async_computation.4 | async-start | bytes 524288 | tf_op jit(solution)/shard_map/psum | solution.py:52
  630.5 597.1 %copy-start.4 = (bf16[3584,64]{0,1:T(8,128)(2,1)S(1)}, bf16[3584,64]{0,1:T(8,128)(2,1)}, u32[]{:S(2)}) copy-start(bf16[3584,64]{0,1:T(8,128)(2,1)} %param.15) | copy-start | bytes 1376260
  1227.6 4.5 copy-start.3
  1227.6 27.3 %copy-start.1 = (f32[64,64]{1,0:T(8,128)S(1)}, f32[64,64]{1,0:T(8,128)}, u32[]{:S(2)}) copy-start(f32[64,64]{1,0:T(8,128)} %param.16) | copy-start | bytes 49156
  1231.4 32.1 %copy-start.2 = (f32[64,64]{1,0:T(8,128)S(1)}, f32[64,64]{1,0:T(8,128)}, u32[]{:S(2)}) copy-start(f32[64,64]{1,0:T(8,128)} %param.17) | copy-start | bytes 49156
  1231.4 83.6 %all-gather.15.cloned.1.call-start = ((), (), s32[]{:S(2)}) async-start(), calls=%async_computation.5 | async-start | bytes 2359296 | tf_op jit(solution)/shard_map/all_gather | solution.py:67
Sparse Core Ops, SparseCore 0:
  8.9 37.1 all-gather.6
  47.7 559.0 all-gather.12
  608.4 34.4 all-gather.8
  644.2 559.0 all-gather.10
  1231.6 31.9 all-reduce.1
  1265.7 49.2 all-gather.14
where the time goes:
time: 1330 us
  waiting for transfers between devices  1230 us (92%)
  matrix products  60.1 us (5%)
  blocking collectives  25 us (2%)
  between operations  13.5 us (1%)
    all_gather x1, waiting for transfers between devices, shards(): lax.all_gather(gate_weight, 'dp', axis=0, tiled=True)  561 us
    all_gather x1, waiting for transfers between devices, shards(): lax.all_gather(down_weight, 'dp', axis=1, tiled=True)  561 us
    all_gather x1, waiting for transfers between devices, shards(): query_piece = lax.all_gather(queries, 'dp', axis=0, tiled=True)  49.5 us
    all_gather x1, waiting for transfers between devices, shards(): lax.all_gather(inputs, 'mp', axis=2, tiled=True)  36.8 us
  transfers between devices with their start and end apart: 6, of which 6 were waited for; matrix products, arithmetic and copies ran while one was open for 2% of the time, Pallas kernels for 0%

commit v1 on v0

v1 whole, which is shorter than its diff:
```python
import functools

import jax
import jax.numpy as jnp
from jax import lax
from jax.experimental import pallas as pl
from jax.experimental.pallas import tpu as pltpu
from jax.sharding import PartitionSpec as P

LANGS = 32
MESH = pl.DeviceIdType.MESH
CORES = 2


def layout(dp, mp, ff_local):
    nz = dp // 2 if dp % 2 == 0 else 1
    if ff_local % (128 * nz):
        nz = 1
    return nz, dp // nz, mp // CORES


def gather_kernel(
    nz, ny, nx, x_ref, g_ref, w_ref, v_ref, xa, ga, wa, va, send, tok_recv, wgt_recv, local
):
    d, m = lax.axis_index("dp"), lax.axis_index("mp")
    z, y = d // ny, d % ny
    x, c = m // CORES, m % CORES
    mp = nx * CORES
    rows, feats = x_ref.shape
    depth, ff = w_ref.shape
    part = ff // nz

    def at(zz, yy, xx, cc):
        return (zz * ny + yy, xx * CORES + cc)

    core = at(z, y, x, 1 - c)
    peers = [at(lax.rem(z + k, nz), y, x, c) for k in range(1, nz)]
    peers += [at(z, lax.rem(y + k, ny), x, c) for k in range(1, ny)]
    peers += [at(z, y, lax.rem(x + k, nx), c) for k in range(1, nx)]
    peers += [core]
    barrier = pltpu.get_barrier_semaphore()
    for peer in peers:
        pl.semaphore_signal(barrier, inc=1, device_id=peer, device_id_type=MESH)
    pl.semaphore_wait(barrier, len(peers))

    own_tok, all_tok = (x_ref, g_ref), (xa, ga)
    pending = []

    def tok_slot(a, zz, mm):
        return all_tok[a].at[
            pl.ds(zz * rows if isinstance(zz, int) else pl.multiple_of(zz * rows, rows), rows),
            pl.ds(pl.multiple_of(mm * feats, feats), feats),
        ]

    def tok_sem(a, zz, mm):
        return tok_recv.at[(a * nz + zz) * mp + mm]

    def wgt_cut(w, zz):
        span = pl.ds(zz * part if isinstance(zz, int) else pl.multiple_of(zz * part, part), part)
        return w_ref.at[:, span] if w == 0 else v_ref.at[span, :]

    def wgt_slot(w, dd):
        span = pl.ds(pl.multiple_of(dd * depth, depth), depth)
        return wa.at[span, :] if w == 0 else va.at[:, span]

    def wgt_sem(w, dd):
        return wgt_recv.at[w * nz * ny + dd]

    def push(conds, src, dst, sem, dev, like):
        copy = pltpu.make_async_remote_copy(
            src_ref=src, dst_ref=dst, send_sem=send.at[len(pending)], recv_sem=sem,
            device_id=dev, device_id_type=MESH,
        )
        copy.start()
        pending.append((conds, like))

    def arrived(slot, sem, dev):
        pltpu.make_async_remote_copy(
            src_ref=slot, dst_ref=slot, send_sem=send.at[0], recv_sem=sem,
            device_id=dev, device_id_type=MESH,
        ).wait_recv()

    has_right, has_left = z < nz - 1, z > 0

    def along_z(conds, a, zz, src, right, left):
        for go, step, edge in ((right, 1, has_right), (left, -1, has_left)):
            if go and nz > 1:

                @pl.when(edge)
                def _():
                    slot, sem = tok_slot(a, zz, m), tok_sem(a, zz, m)
                    push(conds + (edge,), src, slot, sem, at(z + step, y, x, c), x_ref)

    def along_x_core(conds, a, zz, src):
        slot, sem = tok_slot(a, zz, m), tok_sem(a, zz, m)
        for k in range(1, nx):
            push(conds, src, slot, sem, at(z, y, lax.rem(x + k, nx), c), x_ref)
        push(conds, src, slot, sem, core, x_ref)

    def x_to_core(conds, a, zz):
        for k in range(1, nx):
            xx = lax.rem(x + k, nx)
            mm = xx * CORES + c
            arrived(tok_slot(a, zz, mm), tok_sem(a, zz, mm), at(z, y, xx, c))
            push(conds, tok_slot(a, zz, mm), tok_slot(a, zz, mm), tok_sem(a, zz, mm), core, x_ref)

    def along_y(w, zz, src):
        dd = zz * ny + y
        for k in range(1, ny):
            dev = at(z, lax.rem(y + k, ny), x, c)
            push((), src, wgt_slot(w, dd), wgt_sem(w, dd), dev, wgt_cut(w, 0))

    def guarded(conds, fn):
        if conds:
            pl.when(functools.reduce(jnp.logical_and, conds))(fn)
        else:
            fn()

    for a in range(2):
        along_z((), a, z, own_tok[a], True, True)
        for k in range(1, nz):
            zz = lax.rem(z + k, nz)
            dev = at(zz, y, x, c)
            push((), wgt_cut(a, zz), wgt_slot(a, d), wgt_sem(a, d), dev, wgt_cut(a, 0))
    mine = []
    for a in range(2):
        along_x_core((), a, z, own_tok[a])
        along_y(a, z, wgt_cut(a, z))
        for j, (src, dst) in enumerate(
            ((own_tok[a], tok_slot(a, z, m)), (wgt_cut(a, z), wgt_slot(a, d)))
        ):
            copy = pltpu.make_async_copy(src, dst, local.at[a * 2 + j])
            copy.start()
            mine.append(copy)

    late = [((), a, z) for a in range(2)]

    def drain():
        while late:
            conds, a, zz = late.pop(0)
            guarded(conds, functools.partial(x_to_core, conds, a, zz))

    for s in range(1, nz):
        for a in range(2):
            fresh = []
            for cond, zz, near, right in (
                (z >= s, z - s, z - 1, True), (z + s < nz, z + s, z + 1, False)
            ):
                def relay(cond=cond, zz=zz, near=near, right=right):
                    arrived(tok_slot(a, zz, m), tok_sem(a, zz, m), at(near, y, x, c))
                    if s < nz - 1:
                        along_z((cond,), a, zz, tok_slot(a, zz, m), right, not right)
                    along_x_core((cond,), a, zz, tok_slot(a, zz, m))

                pl.when(cond)(relay)
                fresh.append(((cond,), a, zz))
            zz = lax.rem(z - s + nz, nz)
            dd = zz * ny + y
            arrived(wgt_slot(a, dd), wgt_sem(a, dd), at(zz, y, x, c))
            along_y(a, zz, wgt_slot(a, dd))
            drain()
            late.extend(fresh)
    drain()

    for a in range(2):
        for zz in range(nz):
            for k in range(nx):
                mm = k * CORES + 1 - c
                arrived(tok_slot(a, zz, mm), tok_sem(a, zz, mm), core)
            for k in range(1, ny):
                yy = lax.rem(y + k, ny)
                dd = zz * ny + yy
                arrived(wgt_slot(a, dd), wgt_sem(a, dd), at(z, yy, x, c))
    for copy in mine:
        copy.wait()
    for i, (conds, like) in enumerate(pending):
        sent = pltpu.make_async_remote_copy(
            src_ref=like, dst_ref=like, send_sem=send.at[i], recv_sem=tok_recv.at[0],
            device_id=core, device_id_type=MESH,
        )
        guarded(conds, sent.wait_send)


def gather_all(nz, ny, nx, tokens, grads, gate_weight, down_weight):
    rows, feats = tokens.shape
    depth, ff = gate_weight.shape
    mp, dp = nx * CORES, nz * ny
    part = ff // nz
    sends = 2 * (2 * nz + nz * (nx - 1) + nz * nx + nz + nz * ny + 2 * nz * nx) * 2
    shapes = [(nz * rows, mp * feats)] * 2 + [(dp * depth, part), (part, dp * depth)]
    anywhere = pl.BlockSpec(memory_space=pl.ANY)
    return pl.pallas_call(
        functools.partial(gather_kernel, nz, ny, nx),
        out_shape=[jax.ShapeDtypeStruct(s, jnp.bfloat16) for s in shapes],
        in_specs=[anywhere] * 4,
        out_specs=[anywhere] * 4,
        scratch_shapes=[
            pltpu.SemaphoreType.DMA((sends,)),
            pltpu.SemaphoreType.DMA((2 * nz * mp,)),
            pltpu.SemaphoreType.DMA((2 * dp,)),
            pltpu.SemaphoreType.DMA((4,)),
        ],
        compiler_params=pltpu.CompilerParams(collective_id=0, has_side_effects=True),
        name="gather_all",
    )(tokens, grads, gate_weight, down_weight)


def shards(
    inputs, out_grads, gate_weight, down_weight, in_proj, out_proj, in_precond, out_precond,
    queries, languages,
):
    dp, mp = lax.axis_size("dp"), lax.axis_size("mp")
    nz, ny, nx = layout(dp, mp, gate_weight.shape[1])
    local_ex, seq_len, feats = inputs.shape
    rank = in_proj.shape[1]
    per_language = languages.shape[0] * dp // LANGS
    exact = lax.Precision.HIGHEST

    onehot = (languages[None, :] == jnp.arange(LANGS, dtype=jnp.int32)[:, None])
    lang_sum = jnp.dot(
        onehot.astype(jnp.bfloat16), queries, preferred_element_type=jnp.float32
    )
    lang_sum = lax.psum(lang_sum, "dp")
    lang_sum = lax.all_gather(lang_sum, "mp", axis=1, tiled=True)
    lang_sum = lang_sum.reshape(LANGS, rank, rank)
    turned = jnp.einsum("lij,bj->lib", lang_sum, out_precond, precision=exact)
    turned = jnp.einsum("ia,lib->lab", in_precond, turned, precision=exact)
    turned = turned / (seq_len * per_language)

    tok, grd, gate_all, down_all = gather_all(
        nz, ny, nx,
        inputs.reshape(local_ex * seq_len, feats),
        out_grads.reshape(local_ex * seq_len, feats),
        gate_weight, down_weight,
    )
    gate = jnp.dot(tok, gate_all, preferred_element_type=jnp.float32)
    hidden_grad = lax.dot_general(
        grd, down_all, (((1,), (1,)), ((), ())), preferred_element_type=jnp.float32
    )
    up_grad = (hidden_grad * jax.nn.silu(gate)).astype(jnp.bfloat16)
    part = gate_all.shape[1]
    d = lax.axis_index("dp")
    z, y = d // ny, d % ny
    proj = lax.dynamic_slice_in_dim(out_proj, z * part, part, 0)
    out_part = jnp.dot(up_grad, proj, preferred_element_type=jnp.float32)
    in_part = jnp.dot(tok, in_proj, preferred_element_type=jnp.float32)
    cross = jnp.einsum(
        "esa,esb->eab",
        in_part.reshape(nz * local_ex, seq_len, rank),
        out_part.reshape(nz * local_ex, seq_len, rank),
        precision=exact,
    )
    partial = jnp.einsum("eab,lab->el", cross, turned, precision=exact)
    spread = jnp.arange(ny)[None, :, None, None] == y
    spread = jnp.where(spread, partial.reshape(nz, 1, local_ex, LANGS), 0.0)
    total = lax.psum(spread.reshape(dp * local_ex, LANGS), ("dp", "mp"))
    return lax.dynamic_slice_in_dim(total, d * local_ex, local_ex, 0)


def solution(mesh):
    return jax.shard_map(
        shards,
        mesh=mesh,
        in_specs=(
            P("dp", None, "mp"),
            P("dp", None, "mp"),
            P("dp", "mp"),
            P("mp", "dp"),
            P(),
            P("mp", None),
            P(),
            P(),
            P("dp", "mp"),
            P("dp"),
        ),
        out_specs=P("dp", None),
        check_vma=False,
    )
```

time: 1330 us -> 443 us (0.33)
  waiting for transfers between devices: 1230 us -> 0.04 us
  Pallas kernels: 0 us -> 309 us
  blocking collectives: 25 us -> 57.4 us
    all_gather x5 -> x0, waiting for transfers between devices: 1220 us -> none  [the longest x1 561 us: shards(): lax.all_gather(gate_weight, 'dp', axis=0, tiled=True)]
    pallas_call x0 -> x1, Pallas kernels: none -> 309 us  [gather_all(): pl.pallas_call(functools.partial(gather_kernel, nz, ny, nx), out_shape=[j...]
    psum x1, blocking collectives: 5.67 us -> 49.5 us  [shards(): total = lax.psum(spread.reshape(dp * local_ex, LANGS), ('dp', 'mp'))]
    dot_general x9 -> x8, matrix products: 60.1 us -> 60.8 us  [the longest x1 25.7 us: shards(): out_part = jnp.dot(up_grad, proj, preferred_element_type=jnp.float32)]
  transfers between devices with their start and end apart: 6 -> 1, of which waited for: 6 -> 0; matrix products, arithmetic and copies ran while one was open for 2% -> 12% of each run, Pallas kernels for 0% -> 70%
where the time goes in v1:
time: 443 us
  Pallas kernels  309 us (70%)
  matrix products  60.8 us (14%)
  blocking collectives  57.4 us (13%)
  between operations  13.5 us (3%)
    pallas_call x1, Pallas kernels, gather_all(): pl.pallas_call(functools.partial(gather_kernel, nz, ny, nx), out_shape=[j...  309 us
    psum x1, blocking collectives, shards(): total = lax.psum(spread.reshape(dp * local_ex, LANGS), ('dp', 'mp'))  49.5 us
    dot_general x1, matrix products, shards(): out_part = jnp.dot(up_grad, proj, preferred_element_type=jnp.float32)  25.7 us
    dot_general x1, matrix products, shards(): gate = jnp.dot(tok, gate_all, preferred_element_type=jnp.float32)  23.7 us
  transfers between devices with their start and end apart: 1, of which 0 were waited for; matrix products, arithmetic and copies ran while one was open for 12% of the time, Pallas kernels for 70%

profile of v1, /device:TPU:0, one launch (start us, length us, event | category | flops | bytes accessed | tf_op | source)
XLA Modules:
  0.0 442.9 jit_solution(12305639406990951528)
XLA Ops:
  6.5 0.0 copy-start
  6.5 0.0 all-reduce.2.cloned.1.call-start
  6.5 1.8 fusion.15
  8.4 0.0 all-reduce.2.cloned.1.call-update
  8.4 309.2 %gather_all.1 = (bf16[2048,4096]{1,0:T(8,128)(2,1)}, bf16[2048,4096]{1,0:T(8,128)(2,1)}, bf16[4096,896]{1,0:T(8,128)(2,1)}, bf16[896,4096]{1,0:T(8,128)(2,1)}) custom-call(bf16[512,1024]{1,0:T(8,128)(2,1)} %bitcast.32, bf16[512,1024]{1,0:T(8,128)(2,1)} %bitcast.33, bf16[512,3584]{1,0:T(8,128)(2,1)} %w_ref.1, bf16[3584,512]{1,0:T(8,128)(2,1)} %v_ref.1), custom_call_target="tpu_custom_call" | custom-call | tf_op jit(solution)/shard_map/gather_all/pallas_call | solution.py:192
  317.6 0.0 copy-start.2
  317.6 23.7 %fusion.21 = f32[2048,896]{1,0:T(8,128)} fusion(bf16[2048,4096]{1,0:T(8,128)(2,1)} %get-tuple-element.9, bf16[4096,896]{1,0:T(8,128)(2,1)} %get-tuple-element.12), kind=kOutput, calls=%fused_computation.27 | convolution fusion | flops 15032385536 | bytes 31457280 | tf_op jit(solution)/shard_map/dot_general | solution.py:236
  341.3 0.0 copy-done
  341.3 0.0 copy-done.2
  341.3 5.2 %fusion.20 = f32[2048,64]{0,1:T(8,128)S(1)} fusion(bf16[2048,4096]{1,0:T(8,128)(2,1)S(1)} %copy-done.2, bf16[4096,64]{0,1:T(8,128)(2,1)S(1)} %copy-done), kind=kOutput, calls=%fused_computation.26 | convolution fusion | flops 1073741824 | bytes 17825792 | tf_op jit(solution)/shard_map/dot_general | solution.py:246
  346.6 0.1 broadcast_in_dim.30
  346.6 0.0 copy-start.3
  346.6 0.0 copy-start.4
  346.6 0.0 copy-start.1
  346.7 25.7 %fusion = f32[2048,64]{0,1:T(8,128)S(1)} fusion(f32[2048,896]{1,0:T(8,128)} %fusion.21, bf16[2048,4096]{1,0:T(8,128)(2,1)} %get-tuple-element.10, bf16[896,4096]{1,0:T(8,128)(2,1)} %get-tuple-element.11, bf16[3584,64]{0,1:T(8,128)(2,1)} %param.15, s32[]{:T(128)S(6)} %select_n.26), kind=kOutput, calls=%fused_computation.1 | convolution fusion | flops 15278276608 | bytes 32096260 | tf_op jit(solution)/shard_map/dot_general | solution.py:245
  372.4 0.6 fusion.3
  373.0 0.0 all-reduce.2.cloned.1.call-done
  373.0 7.8 %all_gather.3 = f32[32,4096]{1,0:T(8,128)S(1)} all-gather(f32[32,1024]{1,0:T(8,128)} %all-reduce.2.cloned.1.call-done), channel_id=1, replica_groups=mesh['dp'=8,'mp'=4] {'mp'}, dimensions={1}, use_global_device_ids=true | all-gather | bytes 655360 | tf_op jit(solution)/shard_map/all_gather | solution.py:224
  380.8 0.4 reshape.35
  381.3 0.0 copy-done.3
  381.3 1.0 fusion.13
  382.2 0.0 copy-done.4
  382.3 1.8 fusion.11
  384.1 0.9 copy.14
  384.9 0.9 convolution_bitcast_fusion
  385.9 0.1 broadcast_select_fusion
  386.0 49.5 %psum.15 = f32[8,32]{1,0:T(8,128)S(1)} all-reduce(f32[8,32]{1,0:T(8,128)S(1)} %broadcast_select_fusion), channel_id=1, replica_groups=mesh['dp'=8,'mp'=4] {'dp','mp'}, use_global_device_ids=true, to_apply=%region_1.2 | all-reduce | flops 256 | bytes 2048 | tf_op jit(solution)/shard_map/psum | solution.py:256
  435.5 0.5 constant_dynamic-slice_fusion
  436.0 0.0 copy-done.1
  (3 shorter events, 0.0 us)
Async XLA Ops:
  6.5 334.8 %copy-start = (bf16[4096,64]{0,1:T(8,128)(2,1)S(1)}, bf16[4096,64]{0,1:T(8,128)(2,1)}, u32[]{:S(2)}) copy-start(bf16[4096,64]{0,1:T(8,128)(2,1)} %param.14) | copy-start | bytes 1572868
  6.5 366.5 %all-reduce.2.cloned.1.call-start = ((), (), s32[]{:S(2)}) async-start(), calls=%async_computation | async-start | bytes 262144 | tf_op jit(solution)/shard_map/psum | solution.py:223
  317.6 23.8 %copy-start.2 = (bf16[2048,4096]{1,0:T(8,128)(2,1)S(1)}, bf16[2048,4096]{1,0:T(8,128)(2,1)}, u32[]{:S(2)}) copy-start(bf16[2048,4096]{1,0:T(8,128)(2,1)} %get-tuple-element.9) | copy-start | bytes 50331652
  346.6 34.6 %copy-start.3 = (f32[64,64]{1,0:T(8,128)S(1)}, f32[64,64]{1,0:T(8,128)}, u32[]{:S(2)}) copy-start(f32[64,64]{1,0:T(8,128)} %param.17) | copy-start | bytes 49156
  346.6 35.6 %copy-start.4 = (f32[64,64]{1,0:T(8,128)S(1)}, f32[64,64]{1,0:T(8,128)}, u32[]{:S(2)}) copy-start(f32[64,64]{1,0:T(8,128)} %param.16) | copy-start | bytes 49156
  346.6 89.4 %copy-start.1 = (bf16[4096,64]{0,1:T(8,128)(2,1)S(1)}, bf16[4096,64]{0,1:T(8,128)(2,1)}, u32[]{:S(2)}) copy-start(bf16[4096,64]{0,1:T(8,128)(2,1)} %param.14) | copy-start | bytes 1572868
Sparse Core Ops, SparseCore 0:
  10.7 153.7 all-reduce.1

commit v2 on v1

--- a/solution.py
+++ b/solution.py
@@ -20,7 +20,8 @@
 
 
 def gather_kernel(
-    nz, ny, nx, x_ref, g_ref, w_ref, v_ref, xa, ga, wa, va, send, tok_recv, wgt_recv, local
+    nz, ny, nx, x_ref, g_ref, w_ref, v_ref, ip_ref, op_ref, a_out, b_out, xa, ga,
+    wa, va, silu, buf, send, tok_recv, wgt_recv, local, load_sem,
 ):
     d, m = lax.axis_index("dp"), lax.axis_index("mp")
     z, y = d // ny, d % ny
@@ -116,14 +117,18 @@
         else:
             fn()
 
-    for a in range(2):
+    def own_along_z(a):
         along_z((), a, z, own_tok[a], True, True)
+
+    def own_cuts(a):
         for k in range(1, nz):
             zz = lax.rem(z + k, nz)
             dev = at(zz, y, x, c)
             push((), wgt_cut(a, zz), wgt_slot(a, d), wgt_sem(a, d), dev, wgt_cut(a, 0))
+
     mine = []
-    for a in range(2):
+
+    def own_rest(a):
         along_x_core((), a, z, own_tok[a])
         along_y(a, z, wgt_cut(a, z))
         for j, (src, dst) in enumerate(
@@ -133,46 +138,132 @@
             copy.start()
             mine.append(copy)
 
-    late = [((), a, z) for a in range(2)]
+    late = []
 
     def drain():
         while late:
             conds, a, zz = late.pop(0)
             guarded(conds, functools.partial(x_to_core, conds, a, zz))
 
-    for s in range(1, nz):
-        for a in range(2):
-            fresh = []
-            for cond, zz, near, right in (
-                (z >= s, z - s, z - 1, True), (z + s < nz, z + s, z + 1, False)
-            ):
-                def relay(cond=cond, zz=zz, near=near, right=right):
-                    arrived(tok_slot(a, zz, m), tok_sem(a, zz, m), at(near, y, x, c))
-                    if s < nz - 1:
-                        along_z((cond,), a, zz, tok_slot(a, zz, m), right, not right)
-                    along_x_core((cond,), a, zz, tok_slot(a, zz, m))
-
-                pl.when(cond)(relay)
-                fresh.append(((cond,), a, zz))
-            zz = lax.rem(z - s + nz, nz)
-            dd = zz * ny + y
-            arrived(wgt_slot(a, dd), wgt_sem(a, dd), at(zz, y, x, c))
-            along_y(a, zz, wgt_slot(a, dd))
-            drain()
-            late.extend(fresh)
-    drain()
-
-    for a in range(2):
+    def relay_tokens(a, s):
+        fresh = []
+        for cond, zz, near, right in (
+            (z >= s, z - s, z - 1, True), (z + s < nz, z + s, z + 1, False)
+        ):
+            def relay(cond=cond, zz=zz, near=near, right=right):
+                arrived(tok_slot(a, zz, m), tok_sem(a, zz, m), at(near, y, x, c))
+                if s < nz - 1:
+                    along_z((cond,), a, zz, tok_slot(a, zz, m), right, not right)
+                along_x_core((cond,), a, zz, tok_slot(a, zz, m))
+
+            pl.when(cond)(relay)
+            fresh.append(((cond,), a, zz))
+        drain()
+        late.extend(fresh)
+
+    def relay_cuts(w, s):
+        zz = lax.rem(z - s + nz, nz)
+        dd = zz * ny + y
+        arrived(wgt_slot(w, dd), wgt_sem(w, dd), at(zz, y, x, c))
+        along_y(w, zz, wgt_slot(w, dd))
+
+    def rest_of_cuts(w):
+        for zz in range(nz):
+            for k in range(1, ny):
+                yy = lax.rem(y + k, ny)
+                dd = zz * ny + yy
+                arrived(wgt_slot(w, dd), wgt_sem(w, dd), at(z, yy, x, c))
+        mine[2 * w + 1].wait()
+
+    def rest_of_tokens(a):
         for zz in range(nz):
             for k in range(nx):
                 mm = k * CORES + 1 - c
                 arrived(tok_slot(a, zz, mm), tok_sem(a, zz, mm), core)
-            for k in range(1, ny):
-                yy = lax.rem(y + k, ny)
-                dd = zz * ny + yy
-                arrived(wgt_slot(a, dd), wgt_sem(a, dd), at(z, yy, x, c))
-    for copy in mine:
-        copy.wait()
+        mine[2 * a].wait()
+
+    def load(a, e):
+        span = pl.ds(pl.multiple_of(e * rows, rows), rows)
+        return pltpu.make_async_copy(all_tok[a].at[span, :], buf.at[lax.rem(e, 2)], load_sem.at[lax.rem(e, 2)])
+
+    tile = 256
+    whole_tiles, rest = part // tile, part % tile
+
+    def over_examples(a, step):
+        load(a, 0).start()
+
+        @pl.loop(0, nz)
+        def _(e):
+            load(a, e).wait()
+
+            @pl.when(e + 1 < nz)
+            def _():
+                load(a, e + 1).start()
+
+            block = buf.at[lax.rem(e, 2)]
+            out_rows = pl.ds(pl.multiple_of(e * rows, rows), rows)
+            step(block, out_rows)
+
+    def over_tiles(step):
+        if whole_tiles:
+
+            @pl.loop(0, whole_tiles)
+            def _(j):
+                step(pl.ds(pl.multiple_of(j * tile, tile), tile))
+
+        if rest:
+            step(pl.ds(whole_tiles * tile, rest))
+
+    def gate_step(block, out_rows):
+        a_out[out_rows, :] = jnp.dot(block[...], ip_ref[...], preferred_element_type=jnp.float32)
+
+        def cols(span):
+            v = jnp.dot(block[...], wa[:, span], preferred_element_type=jnp.float32)
+            silu[out_rows, span] = v / (1.0 + jnp.exp(-v))
+
+        over_tiles(cols)
+
+    def hidden_step(block, out_rows):
+        b_out[out_rows, :] = jnp.zeros((rows, b_out.shape[1]), jnp.float32)
+
+        def cols(span):
+            grad = lax.dot_general(
+                block[...], va[span, :], (((1,), (1,)), ((), ())),
+                preferred_element_type=jnp.float32,
+            )
+            up = (grad * silu[out_rows, span]).astype(jnp.bfloat16)
+            b_out[out_rows, :] += jnp.dot(up, op_ref[span, :], preferred_element_type=jnp.float32)
+
+        over_tiles(cols)
+
+    own_along_z(0)
+    own_cuts(0)
+    own_rest(0)
+    own_along_z(1)
+    own_cuts(1)
+    own_rest(1)
+    late.append(((), 0, z))
+    for s in range(1, nz):
+        relay_tokens(0, s)
+        relay_cuts(0, s)
+        if s == 1:
+            relay_tokens(1, 1)
+    drain()
+    if nz > 2:
+        relay_tokens(1, 2)
+    rest_of_cuts(0)
+    rest_of_tokens(0)
+    over_examples(0, gate_step)
+    late.append(((), 1, z))
+    for s in range(1, nz):
+        relay_cuts(1, s)
+        if s > 2:
+            relay_tokens(1, s)
+    drain()
+    rest_of_cuts(1)
+    rest_of_tokens(1)
+    over_examples(1, hidden_step)
+
     for i, (conds, like) in enumerate(pending):
         sent = pltpu.make_async_remote_copy(
             src_ref=like, dst_ref=like, send_sem=send.at[i], recv_sem=tok_recv.at[0],
@@ -181,28 +272,93 @@
         guarded(conds, sent.wait_send)
 
 
-def gather_all(nz, ny, nx, tokens, grads, gate_weight, down_weight):
+def factors(nz, ny, nx, tokens, grads, gate_weight, down_weight, in_proj, out_proj):
     rows, feats = tokens.shape
     depth, ff = gate_weight.shape
     mp, dp = nx * CORES, nz * ny
     part = ff // nz
-    sends = 2 * (2 * nz + nz * (nx - 1) + nz * nx + nz + nz * ny + 2 * nz * nx) * 2
-    shapes = [(nz * rows, mp * feats)] * 2 + [(dp * depth, part), (part, dp * depth)]
+    rank = in_proj.shape[1]
+    sends = 2 * (4 * nz + 2 * nz * (nx - 1) + 4 * nz * nx + nz + nz * ny)
     anywhere = pl.BlockSpec(memory_space=pl.ANY)
-    return pl.pallas_call(
+    vmem = pl.BlockSpec(memory_space=pltpu.VMEM)
+    factor = jax.ShapeDtypeStruct((nz * rows, rank), jnp.float32)
+    gathered = jax.ShapeDtypeStruct((nz * rows, mp * feats), jnp.bfloat16)
+    in_part, out_part, _, _ = pl.pallas_call(
         functools.partial(gather_kernel, nz, ny, nx),
-        out_shape=[jax.ShapeDtypeStruct(s, jnp.bfloat16) for s in shapes],
-        in_specs=[anywhere] * 4,
-        out_specs=[anywhere] * 4,
+        out_shape=[factor, factor, gathered, gathered],
+        in_specs=[anywhere] * 4 + [vmem] * 2,
+        out_specs=[vmem] * 2 + [anywhere] * 2,
         scratch_shapes=[
+            pltpu.VMEM((dp * depth, part), jnp.bfloat16),
+            pltpu.VMEM((part, dp * depth), jnp.bfloat16),
+            pltpu.VMEM((nz * rows, part), jnp.float32),
+            pltpu.VMEM((2, rows, mp * feats), jnp.bfloat16),
             pltpu.SemaphoreType.DMA((sends,)),
             pltpu.SemaphoreType.DMA((2 * nz * mp,)),
             pltpu.SemaphoreType.DMA((2 * dp,)),
             pltpu.SemaphoreType.DMA((4,)),
+            pltpu.SemaphoreType.DMA((2,)),
         ],
-        compiler_params=pltpu.CompilerParams(collective_id=0, has_side_effects=True),
-        name="gather_all",
-    )(tokens, grads, gate_weight, down_weight)
+        compiler_params=pltpu.CompilerParams(
+            collective_id=0, has_side_effects=True, vmem_limit_bytes=52 * 2**20
+        ),
+        name="factors",
+    )(tokens, grads, gate_weight, down_weight, in_proj, out_proj)
+    return in_part, out_part
+
+
+def sum_kernel(nz, ny, nx, part_ref, out_ref, slots, send, recv):
+    d, m = lax.axis_index("dp"), lax.axis_index("mp")
+    z, y = d // ny, d % ny
+    mp = nx * CORES
+    count = nz * mp
+    me = z * mp + m
+
+    def device(i):
+        return (i // mp * ny + y, lax.rem(i, mp))
+
+    barrier = pltpu.get_barrier_semaphore()
+    for k in range(1, count):
+        peer = device(lax.rem(me + k, count))
+        pl.semaphore_signal(barrier, inc=1, device_id=peer, device_id_type=MESH)
+    slots[me] = part_ref[...]
+    pl.semaphore_wait(barrier, count - 1)
+
+    def copy(k, to, into):
+        return pltpu.make_async_remote_copy(
+            src_ref=part_ref, dst_ref=slots.at[into], send_sem=send.at[k],
+            recv_sem=recv.at[into], device_id=device(to), device_id_type=MESH,
+        )
+
+    for k in range(1, count):
+        copy(k, lax.rem(me + k, count), me).start()
+    for k in range(1, count):
+        other = lax.rem(me + count - k, count)
+        copy(k, other, other).wait_recv()
+    total = slots[0]
+    for i in range(1, count):
+        total = total + slots[i]
+    out_ref[...] = total
+    for k in range(1, count):
+        copy(k, lax.rem(me + k, count), me).wait_send()
+
+
+def sum_over_parts(nz, ny, nx, tile):
+    count = nz * nx * CORES
+    vmem = pl.BlockSpec(memory_space=pltpu.VMEM)
+    return pl.pallas_call(
+        functools.partial(sum_kernel, nz, ny, nx),
+        out_shape=jax.ShapeDtypeStruct(tile.shape, jnp.float32),
+        in_specs=[vmem],
+        out_specs=vmem,
+        scratch_shapes=[
+            pltpu.VMEM((count,) + tile.shape, jnp.float32),
+            pltpu.SemaphoreType.DMA((count,)),
+            pltpu.SemaphoreType.DMA((count,)),
+        ],
+        compiler_params=pltpu.CompilerParams(collective_id=1, has_side_effects=True),
+        name="sum_over_parts",
+    )(tile)
 
 
 def shards(
@@ -227,23 +383,15 @@
     turned = jnp.einsum("ia,lib->lab", in_precond, turned, precision=exact)
     turned = turned / (seq_len * per_language)
 
-    tok, grd, gate_all, down_all = gather_all(
+    part = gate_weight.shape[1] // nz
+    z = lax.axis_index("dp") // ny
+    in_part, out_part = factors(
         nz, ny, nx,
         inputs.reshape(local_ex * seq_len, feats),
         out_grads.reshape(local_ex * seq_len, feats),
-        gate_weight, down_weight,
+        gate_weight, down_weight, in_proj,
+        lax.dynamic_slice_in_dim(out_proj, z * part, part, 0),
     )
-    gate = jnp.dot(tok, gate_all, preferred_element_type=jnp.float32)
-    hidden_grad = lax.dot_general(
-        grd, down_all, (((1,), (1,)), ((), ())), preferred_element_type=jnp.float32
-    )
-    up_grad = (hidden_grad * jax.nn.silu(gate)).astype(jnp.bfloat16)
-    part = gate_all.shape[1]
-    d = lax.axis_index("dp")
-    z, y = d // ny, d % ny
-    proj = lax.dynamic_slice_in_dim(out_proj, z * part, part, 0)
-    out_part = jnp.dot(up_grad, proj, preferred_element_type=jnp.float32)
-    in_part = jnp.dot(tok, in_proj, preferred_element_type=jnp.float32)
     cross = jnp.einsum(
         "esa,esb->eab",
         in_part.reshape(nz * local_ex, seq_len, rank),
@@ -251,10 +399,10 @@
         precision=exact,
     )
     partial = jnp.einsum("eab,lab->el", cross, turned, precision=exact)
-    spread = jnp.arange(ny)[None, :, None, None] == y
-    spread = jnp.where(spread, partial.reshape(nz, 1, local_ex, LANGS), 0.0)
-    total = lax.psum(spread.reshape(dp * local_ex, LANGS), ("dp", "mp"))
-    return lax.dynamic_slice_in_dim(total, d * local_ex, local_ex, 0)
+    held = nz * local_ex
+    tile = jnp.pad(partial, ((0, -held % 8), (0, -LANGS % 128)))
+    total = sum_over_parts(nz, ny, nx, tile)[:, :LANGS]
+    return lax.dynamic_slice_in_dim(total, z * local_ex, local_ex, 0)
 
 
 def solution(mesh):

time: 443 us -> 444 us (level)
  Pallas kernels: 309 us -> 408 us
  matrix products: 60.8 us -> 8.63 us
  blocking collectives: 57.4 us -> 7.97 us
    pallas_call x1 -> x2, Pallas kernels: 309 us -> 408 us  [the longest x1 399 us: factors(): pl.pallas_call(functools.partial(gather_kernel, nz, ny, nx), out_shape=[f...]
    dot_general x3 -> x0, matrix products: 54.6 us -> none  [the longest x1 25.7 us: shards(): out_part = jnp.dot(up_grad, proj, preferred_element_type=jnp.float32)]
    psum x1 -> x0, blocking collectives: 49.5 us -> none  [shards(): total = lax.psum(spread.reshape(dp * local_ex, LANGS), ('dp', 'mp'))]
  transfers between devices with their start and end apart: 1 -> 1, of which waited for: 0 -> 0; matrix products, arithmetic and copies ran while one was open for 12% -> 1% of each run, Pallas kernels for 70% -> 90%
where the time goes in v2:
time: 444 us
  Pallas kernels  408 us (92%)
  between operations  13.5 us (3%)
  matrix products  8.63 us (2%)
  blocking collectives  7.97 us (2%)
  local copies, waits for them, and re-layouts  5.71 us (1%)
    pallas_call x1, Pallas kernels, factors(): pl.pallas_call(functools.partial(gather_kernel, nz, ny, nx), out_shape=[f...  399 us
  transfers between devices with their start and end apart: 1, of which 0 were waited for; matrix products, arithmetic and copies ran while one was open for 1% of the time, Pallas kernels for 90%

profile of v2, /device:TPU:0, one launch (start us, length us, event | category | flops | bytes accessed | tf_op | source)
XLA Modules:
  0.0 443.6 jit_solution(11678537354755106051)
XLA Ops:
  6.5 0.0 copy-start
  6.5 0.0 copy-start.1
  6.5 0.0 copy-start.2
  6.5 0.0 all-reduce.3.cloned.1.call-start
  6.5 1.8 fusion.8
  8.4 0.0 all-reduce.3.cloned.1.call-update
  8.4 0.0 copy-done
  8.5 0.2 copy.15.op_ref
  8.6 2.4 copy.12.ip_ref
  11.0 399.4 %factors.1 = (f32[2048,64]{1,0:T(8,128)S(1)}, f32[2048,64]{1,0:T(8,128)}, bf16[2048,4096]{1,0:T(8,128)(2,1)}, bf16[2048,4096]{1,0:T(8,128)(2,1)}) custom-call(bf16[512,1024]{1,0:T(8,128)(2,1)} %bitcast.23, bf16[512,1024]{1,0:T(8,128)(2,1)} %bitcast.24, bf16[512,3584]{1,0:T(8,128)(2,1)} %w_ref.1, bf16[3584,512]{1,0:T(8,128)(2,1)} %v_ref.1, ...), custom_call_target="tpu_custom_call" | custom-call | tf_op jit(solution)/shard_map/factors/pallas_call | solution.py:286
  410.4 3.1 fusion.11
  413.5 0.0 all-reduce.3.cloned.1.call-done
  413.5 8.0 %all_gather.3 = f32[32,4096]{1,0:T(8,128)S(1)} all-gather(f32[32,1024]{1,0:T(8,128)} %all-reduce.3.cloned.1.call-done), channel_id=1, replica_groups=mesh['dp'=8,'mp'=4] {'mp'}, dimensions={1}, use_global_device_ids=true | all-gather | bytes 655360 | tf_op jit(solution)/shard_map/all_gather | solution.py:380
  421.5 0.4 reshape.20
  421.9 0.0 copy-done.1
  421.9 1.0 fusion.6
  422.9 0.0 copy-done.2
  422.9 1.8 fusion.4
  424.7 0.9 copy.14
  425.6 0.9 convolution_bitcast_fusion
  426.6 0.6 pad.4.part_ref
  427.2 8.4 %sum_over_parts.1 = f32[8,128]{1,0:T(8,128)} custom-call(f32[8,128]{1,0:T(8,128)} %pad.4.part_ref), custom_call_target="tpu_custom_call" | custom-call | tf_op jit(solution)/shard_map/sum_over_parts/pallas_call | solution.py:349
  435.6 1.2 constant_dynamic-slice_fusion
  (1 shorter events, 0.0 us)
Async XLA Ops:
  6.5 1.9 copy-start
  6.5 415.4 %copy-start.1 = (f32[64,64]{1,0:T(8,128)S(1)}, f32[64,64]{1,0:T(8,128)}, u32[]{:S(2)}) copy-start(f32[64,64]{1,0:T(8,128)} %param.17) | copy-start | bytes 49156
  6.5 416.4 %copy-start.2 = (f32[64,64]{1,0:T(8,128)S(1)}, f32[64,64]{1,0:T(8,128)}, u32[]{:S(2)}) copy-start(f32[64,64]{1,0:T(8,128)} %param.16) | copy-start | bytes 49156
  6.5 407.0 %all-reduce.3.cloned.1.call-start = ((), (), s32[]{:S(2)}) async-start(), calls=%async_computation | async-start | bytes 262144 | tf_op jit(solution)/shard_map/psum | solution.py:379
Sparse Core Ops, SparseCore 0:
  10.7 165.2 all-reduce.2

commit v3 on v2

--- a/solution.py
+++ b/solution.py
@@ -10,6 +10,7 @@
 LANGS = 32
 MESH = pl.DeviceIdType.MESH
 CORES = 2
+TILE = 256
 
 
 def layout(dp, mp, ff_local):
@@ -17,6 +18,12 @@
     if ff_local % (128 * nz):
         nz = 1
     return nz, dp // nz, mp // CORES
+
+
+def cuts_of(part):
+    first = min(part, (part // 2 + TILE - 1) // TILE * TILE)
+    spans = [(0, part), (0, first)]
+    return spans + [(first, part - first)] if first < part else spans
 
 
 def gather_kernel(
@@ -30,6 +37,7 @@
     rows, feats = x_ref.shape
     depth, ff = w_ref.shape
     part = ff // nz
+    cut_spans = cuts_of(part)
 
     def at(zz, yy, xx, cc):
         return (zz * ny + yy, xx * CORES + cc)
@@ -57,12 +65,14 @@
         return tok_recv.at[(a * nz + zz) * mp + mm]
 
     def wgt_cut(w, zz):
-        span = pl.ds(zz * part if isinstance(zz, int) else pl.multiple_of(zz * part, part), part)
+        lo, size = cut_spans[w]
+        span = pl.ds(zz * part + lo if isinstance(zz, int) else pl.multiple_of(zz * part + lo, 128), size)
         return w_ref.at[:, span] if w == 0 else v_ref.at[span, :]
 
     def wgt_slot(w, dd):
+        lo, size = cut_spans[w]
         span = pl.ds(pl.multiple_of(dd * depth, depth), depth)
-        return wa.at[span, :] if w == 0 else va.at[:, span]
+        return wa.at[span, pl.ds(0, part)] if w == 0 else va.at[pl.ds(lo, size), span]
 
     def wgt_sem(w, dd):
         return wgt_recv.at[w * nz * ny + dd]
@@ -126,17 +136,20 @@
             dev = at(zz, y, x, c)
             push((), wgt_cut(a, zz), wgt_slot(a, d), wgt_sem(a, d), dev, wgt_cut(a, 0))
 
-    mine = []
-
-    def own_rest(a):
+    own_copies = {}
+
+    def keep(key, src, dst):
+        own_copies[key] = pltpu.make_async_copy(src, dst, local.at[len(own_copies)])
+        own_copies[key].start()
+
+    def own_tokens(a):
         along_x_core((), a, z, own_tok[a])
-        along_y(a, z, wgt_cut(a, z))
-        for j, (src, dst) in enumerate(
-            ((own_tok[a], tok_slot(a, z, m)), (wgt_cut(a, z), wgt_slot(a, d)))
-        ):
-            copy = pltpu.make_async_copy(src, dst, local.at[a * 2 + j])
-            copy.start()
-            mine.append(copy)
+        keep(("tokens", a), own_tok[a], tok_slot(a, z, m))
+        late.append(((), a, z))
+
+    def own_weights(w):
+        along_y(w, z, wgt_cut(w, z))
+        keep(("cut", w), wgt_cut(w, z), wgt_slot(w, d))
 
     late = []
 
@@ -173,58 +186,59 @@
                 yy = lax.rem(y + k, ny)
                 dd = zz * ny + yy
                 arrived(wgt_slot(w, dd), wgt_sem(w, dd), at(z, yy, x, c))
-        mine[2 * w + 1].wait()
+        own_copies["cut", w].wait()
 
     def rest_of_tokens(a):
         for zz in range(nz):
             for k in range(nx):
                 mm = k * CORES + 1 - c
                 arrived(tok_slot(a, zz, mm), tok_sem(a, zz, mm), core)
-        mine[2 * a].wait()
+        own_copies["tokens", a].wait()
 
     def load(a, e):
-        span = pl.ds(pl.multiple_of(e * rows, rows), rows)
-        return pltpu.make_async_copy(all_tok[a].at[span, :], buf.at[lax.rem(e, 2)], load_sem.at[lax.rem(e, 2)])
-
-    tile = 256
-    whole_tiles, rest = part // tile, part % tile
-
-    def over_examples(a, step):
-        load(a, 0).start()
-
-        @pl.loop(0, nz)
-        def _(e):
-            load(a, e).wait()
-
-            @pl.when(e + 1 < nz)
-            def _():
-                load(a, e + 1).start()
-
-            block = buf.at[lax.rem(e, 2)]
-            out_rows = pl.ds(pl.multiple_of(e * rows, rows), rows)
-            step(block, out_rows)
-
-    def over_tiles(step):
-        if whole_tiles:
-
-            @pl.loop(0, whole_tiles)
+        return pltpu.make_async_copy(
+            all_tok[a].at[pl.ds(e * rows, rows), :], buf.at[e % 2], load_sem.at[e % 2]
+        )
+
+    def example(a, e):
+        if e == 0:
+            load(a, 0).start()
+        load(a, e).wait()
+        if e + 1 < nz:
+            load(a, e + 1).start()
+        return buf.at[e % 2], pl.ds(e * rows, rows)
+
+    def over_tiles(lo, size, step):
+        whole = size // TILE
+        if whole:
+
+            @pl.loop(0, whole)
             def _(j):
-                step(pl.ds(pl.multiple_of(j * tile, tile), tile))
-
-        if rest:
-            step(pl.ds(whole_tiles * tile, rest))
-
-    def gate_step(block, out_rows):
-        a_out[out_rows, :] = jnp.dot(block[...], ip_ref[...], preferred_element_type=jnp.float32)
+                step(pl.ds(pl.multiple_of(lo + j * TILE, TILE), TILE))
+
+        if size % TILE:
+            step(pl.ds(lo + whole * TILE, size % TILE))
+
+    def gate_step(e):
+        block, out_rows = example(0, e)
+        last = part // TILE * TILE
+        wide = part - last
 
         def cols(span):
             v = jnp.dot(block[...], wa[:, span], preferred_element_type=jnp.float32)
             silu[out_rows, span] = v / (1.0 + jnp.exp(-v))
 
-        over_tiles(cols)
-
-    def hidden_step(block, out_rows):
-        b_out[out_rows, :] = jnp.zeros((rows, b_out.shape[1]), jnp.float32)
+        over_tiles(0, last, cols)
+        v = jnp.dot(block[...], wa[:, last:], preferred_element_type=jnp.float32)
+        if wide:
+            gate = v[:, :wide]
+            silu[out_rows, last:part] = gate / (1.0 + jnp.exp(-gate))
+        a_out[out_rows, :] = v[:, wide:]
+
+    def hidden_step(w, e):
+        block, out_rows = example(1, e)
+        if w == 1:
+            b_out[out_rows, :] = jnp.zeros((rows, b_out.shape[1]), jnp.float32)
 
         def cols(span):
             grad = lax.dot_general(
@@ -234,35 +248,43 @@
             up = (grad * silu[out_rows, span]).astype(jnp.bfloat16)
             b_out[out_rows, :] += jnp.dot(up, op_ref[span, :], preferred_element_type=jnp.float32)
 
-        over_tiles(cols)
+        over_tiles(*cut_spans[w], cols)
 
     own_along_z(0)
+    own_along_z(1)
+    own_tokens(0)
+    own_tokens(1)
     own_cuts(0)
-    own_rest(0)
-    own_along_z(1)
-    own_cuts(1)
-    own_rest(1)
-    late.append(((), 0, z))
+    own_weights(0)
+    wa[:, part:] = ip_ref[...]
+    down = range(1, len(cut_spans))
     for s in range(1, nz):
         relay_tokens(0, s)
-        relay_cuts(0, s)
+        relay_tokens(1, s)
         if s == 1:
-            relay_tokens(1, 1)
+            for w in down:
+                own_cuts(w)
+        if s > 1:
+            relay_cuts(0, s - 1)
+    for w in down:
+        own_weights(w)
+    if nz > 1:
+        relay_cuts(0, nz - 1)
     drain()
-    if nz > 2:
-        relay_tokens(1, 2)
     rest_of_cuts(0)
     rest_of_tokens(0)
-    over_examples(0, gate_step)
-    late.append(((), 1, z))
-    for s in range(1, nz):
-        relay_cuts(1, s)
-        if s > 2:
-            relay_tokens(1, s)
-    drain()
-    rest_of_cuts(1)
+    steps = [(w, s) for w in down for s in range(1, nz)]
+    for e in range(nz):
+        gate_step(e)
+        if e < nz - 1:
+            relay_cuts(*steps.pop(0))
+    for w, s in steps:
+        relay_cuts(w, s)
     rest_of_tokens(1)
-    over_examples(1, hidden_step)
+    for w in down:
+        rest_of_cuts(w)
+        for e in range(nz):
+            hidden_step(w, e)
 
     for i, (conds, like) in enumerate(pending):
         sent = pltpu.make_async_remote_copy(
@@ -278,33 +300,36 @@
     mp, dp = nx * CORES, nz * ny
     part = ff // nz
     rank = in_proj.shape[1]
-    sends = 2 * (4 * nz + 2 * nz * (nx - 1) + 4 * nz * nx + nz + nz * ny)
+    sends = 2 * (4 * nz + 2 * nz * (nx - 1) + 4 * nz * nx) + 3 * (nz + nz * ny)
+    in_wide = jnp.pad(in_proj, ((0, 0), (0, -rank % 128)))
+    wide = in_wide.shape[1]
     anywhere = pl.BlockSpec(memory_space=pl.ANY)
     vmem = pl.BlockSpec(memory_space=pltpu.VMEM)
-    factor = jax.ShapeDtypeStruct((nz * rows, rank), jnp.float32)
+    in_factor = jax.ShapeDtypeStruct((nz * rows, wide), jnp.float32)
+    out_factor = jax.ShapeDtypeStruct((nz * rows, rank), jnp.float32)
     gathered = jax.ShapeDtypeStruct((nz * rows, mp * feats), jnp.bfloat16)
     in_part, out_part, _, _ = pl.pallas_call(
         functools.partial(gather_kernel, nz, ny, nx),
-        out_shape=[factor, factor, gathered, gathered],
+        out_shape=[in_factor, out_factor, gathered, gathered],
         in_specs=[anywhere] * 4 + [vmem] * 2,
         out_specs=[vmem] * 2 + [anywhere] * 2,
         scratch_shapes=[
-            pltpu.VMEM((dp * depth, part), jnp.bfloat16),
+            pltpu.VMEM((dp * depth, part + wide), jnp.bfloat16),
             pltpu.VMEM((part, dp * depth), jnp.bfloat16),
             pltpu.VMEM((nz * rows, part), jnp.float32),
             pltpu.VMEM((2, rows, mp * feats), jnp.bfloat16),
             pltpu.SemaphoreType.DMA((sends,)),
             pltpu.SemaphoreType.DMA((2 * nz * mp,)),
-            pltpu.SemaphoreType.DMA((2 * dp,)),
-            pltpu.SemaphoreType.DMA((4,)),
+            pltpu.SemaphoreType.DMA((3 * dp,)),
+            pltpu.SemaphoreType.DMA((5,)),
             pltpu.SemaphoreType.DMA((2,)),
         ],
         compiler_params=pltpu.CompilerParams(
             collective_id=0, has_side_effects=True, vmem_limit_bytes=52 * 2**20
         ),
         name="factors",
-    )(tokens, grads, gate_weight, down_weight, in_proj, out_proj)
-    return in_part, out_part
+    )(tokens, grads, gate_weight, down_weight, in_wide, out_proj)
+    return in_part[:, :rank], out_part
 
 
 def sum_kernel(nz, ny, nx, part_ref, out_ref, slots, send, recv):

time: 444 us -> 459 us (1.034)
  Pallas kernels: 408 us -> 423 us
    pallas_call x1, Pallas kernels: 399 us -> 415 us  [factors(): pl.pallas_call(functools.partial(gather_kernel, nz, ny, nx), out_shape=[i...]
where the time goes in v3:
time: 459 us; the launch traced here: 458 us
  Pallas kernels  423 us (92%)
  between operations  13.5 us (3%)
  matrix products  8.63 us (2%)
  blocking collectives  7.59 us (2%)
  local copies, waits for them, and re-layouts  6.05 us (1%)
    pallas_call x1, Pallas kernels, factors(): pl.pallas_call(functools.partial(gather_kernel, nz, ny, nx), out_shape=[i...  415 us
  transfers between devices with their start and end apart: 1, of which 0 were waited for; matrix products, arithmetic and copies ran while one was open for 1% of the time, Pallas kernels for 90%

profile of v3, /device:TPU:0, one launch (start us, length us, event | category | flops | bytes accessed | tf_op | source)
XLA Modules:
  0.0 458.5 jit_solution(6999406683342405751)
XLA Ops:
  6.5 0.0 copy-start
  6.5 0.0 copy-start.1
  6.5 0.0 copy-start.2
  6.5 0.0 all-reduce.4.cloned.1.call-start
  6.5 1.8 fusion.8
  8.4 0.0 all-reduce.4.cloned.1.call-update
  8.4 0.0 copy-done
  8.5 0.2 copy.15.op_ref
  8.6 1.5 copy.11
  10.2 1.2 pad.8.ip_ref
  11.3 414.7 %factors.1 = (f32[2048,128]{1,0:T(8,128)S(1)}, f32[2048,64]{1,0:T(8,128)}, bf16[2048,4096]{1,0:T(8,128)(2,1)}, bf16[2048,4096]{1,0:T(8,128)(2,1)}) custom-call(bf16[512,1024]{1,0:T(8,128)(2,1)} %bitcast.24, bf16[512,1024]{1,0:T(8,128)(2,1)} %bitcast.25, bf16[512,3584]{1,0:T(8,128)(2,1)} %w_ref.1, bf16[3584,512]{1,0:T(8,128)(2,1)} %v_ref.1, ...), custom_call_target="tpu_custom_call" | custom-call | tf_op jit(solution)/shard_map/factors/pallas_call | solution.py:311
  426.1 3.1 fusion.11
  429.2 0.0 all-reduce.4.cloned.1.call-done
  429.2 7.6 %all_gather.3 = f32[32,4096]{1,0:T(8,128)S(1)} all-gather(f32[32,1024]{1,0:T(8,128)} %all-reduce.4.cloned.1.call-done), channel_id=1, replica_groups=mesh['dp'=8,'mp'=4] {'mp'}, dimensions={1}, use_global_device_ids=true | all-gather | bytes 655360 | tf_op jit(solution)/shard_map/all_gather | solution.py:405
  436.8 0.4 reshape.20
  437.2 0.0 copy-done.1
  437.2 1.0 fusion.6
  438.2 0.0 copy-done.2
  438.2 1.8 fusion.4
  440.0 0.9 copy.14
  441.0 0.9 convolution_bitcast_fusion
  441.9 0.6 pad.9.part_ref
  442.5 7.9 %sum_over_parts.1 = f32[8,128]{1,0:T(8,128)} custom-call(f32[8,128]{1,0:T(8,128)} %pad.9.part_ref), custom_call_target="tpu_custom_call" | custom-call | tf_op jit(solution)/shard_map/sum_over_parts/pallas_call | solution.py:374
  450.4 1.2 constant_dynamic-slice_fusion
  (1 shorter events, 0.0 us)
Async XLA Ops:
  6.5 1.9 copy-start
  6.5 430.7 %copy-start.1 = (f32[64,64]{1,0:T(8,128)S(1)}, f32[64,64]{1,0:T(8,128)}, u32[]{:S(2)}) copy-start(f32[64,64]{1,0:T(8,128)} %param.17) | copy-start | bytes 49156
  6.5 431.7 %copy-start.2 = (f32[64,64]{1,0:T(8,128)S(1)}, f32[64,64]{1,0:T(8,128)}, u32[]{:S(2)}) copy-start(f32[64,64]{1,0:T(8,128)} %param.16) | copy-start | bytes 49156
  6.5 422.7 %all-reduce.4.cloned.1.call-start = ((), (), s32[]{:S(2)}) async-start(), calls=%async_computation | async-start | bytes 262144 | tf_op jit(solution)/shard_map/psum | solution.py:404
Sparse Core Ops, SparseCore 0:
  10.7 98.7 all-reduce.3

commit v4 on v1

--- a/solution.py
+++ b/solution.py
@@ -118,10 +118,11 @@
 
     for a in range(2):
         along_z((), a, z, own_tok[a], True, True)
+    for w in range(2):
         for k in range(1, nz):
             zz = lax.rem(z + k, nz)
             dev = at(zz, y, x, c)
-            push((), wgt_cut(a, zz), wgt_slot(a, d), wgt_sem(a, d), dev, wgt_cut(a, 0))
+            push((), wgt_cut(w, zz), wgt_slot(w, d), wgt_sem(w, d), dev, wgt_cut(w, 0))
     mine = []
     for a in range(2):
         along_x_core((), a, z, own_tok[a])
@@ -135,14 +136,20 @@
 
     late = [((), a, z) for a in range(2)]
 
-    def drain():
-        while late:
+    def drain(keep):
+        while len(late) > keep:
             conds, a, zz = late.pop(0)
             guarded(conds, functools.partial(x_to_core, conds, a, zz))
 
+    def relay_cuts(s):
+        zz = lax.rem(z - s + nz, nz)
+        dd = zz * ny + y
+        for w in range(2):
+            arrived(wgt_slot(w, dd), wgt_sem(w, dd), at(zz, y, x, c))
+            along_y(w, zz, wgt_slot(w, dd))
+
     for s in range(1, nz):
         for a in range(2):
-            fresh = []
             for cond, zz, near, right in (
                 (z >= s, z - s, z - 1, True), (z + s < nz, z + s, z + 1, False)
             ):
@@ -153,14 +160,13 @@
                     along_x_core((cond,), a, zz, tok_slot(a, zz, m))
 
                 pl.when(cond)(relay)
-                fresh.append(((cond,), a, zz))
-            zz = lax.rem(z - s + nz, nz)
-            dd = zz * ny + y
-            arrived(wgt_slot(a, dd), wgt_sem(a, dd), at(zz, y, x, c))
-            along_y(a, zz, wgt_slot(a, dd))
-            drain()
-            late.extend(fresh)
-    drain()
+                late.append(((cond,), a, zz))
+        if s > 1:
+            relay_cuts(s - 1)
+        drain(4)
+    if nz > 1:
+        relay_cuts(nz - 1)
+    drain(0)
 
     for a in range(2):
         for zz in range(nz):
@@ -205,6 +211,60 @@
     )(tokens, grads, gate_weight, down_weight)
 
 
+def sum_kernel(nz, ny, nx, part_ref, out_ref, slots, send, recv):
+    d, m = lax.axis_index("dp"), lax.axis_index("mp")
+    z, y = d // ny, d % ny
+    mp = nx * CORES
+    count = nz * mp
+    me = z * mp + m
+
+    def device(i):
+        return (i // mp * ny + y, lax.rem(i, mp))
+
+    barrier = pltpu.get_barrier_semaphore()
+    for k in range(1, count):
+        peer = device(lax.rem(me + k, count))
+        pl.semaphore_signal(barrier, inc=1, device_id=peer, device_id_type=MESH)
+    slots[me] = part_ref[...]
+    pl.semaphore_wait(barrier, count - 1)
+
+    def copy(k, to, into):
+        return pltpu.make_async_remote_copy(
+            src_ref=part_ref, dst_ref=slots.at[into], send_sem=send.at[k],
+            recv_sem=recv.at[into], device_id=device(to), device_id_type=MESH,
+        )
+
+    for k in range(1, count):
+        copy(k, lax.rem(me + k, count), me).start()
+    for k in range(1, count):
+        other = lax.rem(me + count - k, count)
+        copy(k, other, other).wait_recv()
+    total = slots[0]
+    for i in range(1, count):
+        total = total + slots[i]
+    out_ref[...] = total
+    for k in range(1, count):
+        copy(k, lax.rem(me + k, count), me).wait_send()
+
+
+def sum_over_parts(nz, ny, nx, tile):
+    count = nz * nx * CORES
+    vmem = pl.BlockSpec(memory_space=pltpu.VMEM)
+    return pl.pallas_call(
+        functools.partial(sum_kernel, nz, ny, nx),
+        out_shape=jax.ShapeDtypeStruct(tile.shape, jnp.float32),
+        in_specs=[vmem],
+        out_specs=vmem,
+        scratch_shapes=[
+            pltpu.VMEM((count,) + tile.shape, jnp.float32),
+            pltpu.SemaphoreType.DMA((count,)),
+            pltpu.SemaphoreType.DMA((count,)),
+        ],
+        compiler_params=pltpu.CompilerParams(collective_id=1, has_side_effects=True),
+        name="sum_over_parts",
+    )(tile)
+
+
 def shards(
     inputs, out_grads, gate_weight, down_weight, in_proj, out_proj, in_precond, out_precond,
     queries, languages,
@@ -221,8 +281,13 @@
         onehot.astype(jnp.bfloat16), queries, preferred_element_type=jnp.float32
     )
     lang_sum = lax.psum(lang_sum, "dp")
-    lang_sum = lax.all_gather(lang_sum, "mp", axis=1, tiled=True)
-    lang_sum = lang_sum.reshape(LANGS, rank, rank)
+    m = lax.axis_index("mp")
+    blocks = jnp.zeros((mp,) + lang_sum.shape, jnp.float32)
+    for k in range(mp):
+        ring = [(i, (i + k) % mp) for i in range(mp)]
+        block = lax.ppermute(lang_sum, "mp", ring) if k else lang_sum
+        blocks = lax.dynamic_update_index_in_dim(blocks, block, lax.rem(m + mp - k, mp), 0)
+    lang_sum = blocks.swapaxes(0, 1).reshape(LANGS, rank, rank)
     turned = jnp.einsum("lij,bj->lib", lang_sum, out_precond, precision=exact)
     turned = jnp.einsum("ia,lib->lab", in_precond, turned, precision=exact)
     turned = turned / (seq_len * per_language)
@@ -240,7 +305,7 @@
     up_grad = (hidden_grad * jax.nn.silu(gate)).astype(jnp.bfloat16)
     part = gate_all.shape[1]
     d = lax.axis_index("dp")
-    z, y = d // ny, d % ny
+    z = d // ny
     proj = lax.dynamic_slice_in_dim(out_proj, z * part, part, 0)
     out_part = jnp.dot(up_grad, proj, preferred_element_type=jnp.float32)
     in_part = jnp.dot(tok, in_proj, preferred_element_type=jnp.float32)
@@ -251,10 +316,10 @@
         precision=exact,
     )
     partial = jnp.einsum("eab,lab->el", cross, turned, precision=exact)
-    spread = jnp.arange(ny)[None, :, None, None] == y
-    spread = jnp.where(spread, partial.reshape(nz, 1, local_ex, LANGS), 0.0)
-    total = lax.psum(spread.reshape(dp * local_ex, LANGS), ("dp", "mp"))
-    return lax.dynamic_slice_in_dim(total, d * local_ex, local_ex, 0)
+    held = nz * local_ex
+    tile = jnp.pad(partial, ((0, -held % 8), (0, -LANGS % 128)))
+    total = sum_over_parts(nz, ny, nx, tile)[:, :LANGS]
+    return lax.dynamic_slice_in_dim(total, z * local_ex, local_ex, 0)
 
 
 def solution(mesh):

time: 443 us -> 481 us (1.086)
  Pallas kernels: 309 us -> 387 us
  blocking collectives: 57.4 us -> 0 us
  local copies, waits for them, and re-layouts: 1.92 us -> 9 us
  matrix products: 60.8 us -> 66.4 us
    pallas_call x1, Pallas kernels: 309 us -> 363 us  [gather_all(): pl.pallas_call(functools.partial(gather_kernel, nz, ny, nx), out_shape=[j...]
    psum x1 -> x0, blocking collectives: 49.5 us -> none  [shards(): total = lax.psum(spread.reshape(dp * local_ex, LANGS), ('dp', 'mp'))]
    pallas_call x0 -> x1, Pallas kernels: none -> 24.2 us  [sum_over_parts(): pl.pallas_call(functools.partial(sum_kernel, nz, ny, nx), out_shape=jax.S...]
    all_gather x1 -> x0, blocking collectives: 7.83 us -> none  [shards(): lang_sum = lax.all_gather(lang_sum, 'mp', axis=1, tiled=True)]
    dot_general x1, matrix products: 5.18 us -> 11 us  [shards(): in_part = jnp.dot(tok, in_proj, preferred_element_type=jnp.float32)]
  transfers between devices with their start and end apart: 1 -> 4, of which waited for: 0 -> 2; matrix products, arithmetic and copies ran while one was open for 12% -> 13% of each run, Pallas kernels for 70% -> 75%
where the time goes in v4:
time: 481 us
  Pallas kernels  387 us (80%)
  matrix products  66.4 us (14%)
  between operations  13.6 us (3%)
  local copies, waits for them, and re-layouts  9 us (2%)
    pallas_call x1, Pallas kernels, gather_all(): pl.pallas_call(functools.partial(gather_kernel, nz, ny, nx), out_shape=[j...  363 us
    dot_general x1, matrix products, shards(): out_part = jnp.dot(up_grad, proj, preferred_element_type=jnp.float32)  25.7 us
    pallas_call x1, Pallas kernels, sum_over_parts(): pl.pallas_call(functools.partial(sum_kernel, nz, ny, nx), out_shape=jax.S...  24.2 us
    dot_general x1, matrix products, shards(): gate = jnp.dot(tok, gate_all, preferred_element_type=jnp.float32)  23.6 us
    dot_general x1, matrix products, shards(): in_part = jnp.dot(tok, in_proj, preferred_element_type=jnp.float32)  11 us
  transfers between devices with their start and end apart: 4, of which 2 were waited for; matrix products, arithmetic and copies ran while one was open for 13% of the time, Pallas kernels for 75%

profile of v4, /device:TPU:0, one launch (start us, length us, event | category | flops | bytes accessed | tf_op | source)
XLA Modules:
  0.0 480.8 jit_solution(1985208557054549797)
XLA Ops:
  6.5 0.0 copy-start
  6.5 0.0 all-reduce.3.cloned.1.call-start
  6.5 1.8 fusion.15
  8.4 0.0 all-reduce.3.cloned.1.call-update
  8.4 362.8 %gather_all.1 = (bf16[2048,4096]{1,0:T(8,128)(2,1)}, bf16[2048,4096]{1,0:T(8,128)(2,1)}, bf16[4096,896]{1,0:T(8,128)(2,1)}, bf16[896,4096]{1,0:T(8,128)(2,1)}) custom-call(bf16[512,1024]{1,0:T(8,128)(2,1)} %bitcast.38, bf16[512,1024]{1,0:T(8,128)(2,1)} %bitcast.39, bf16[512,3584]{1,0:T(8,128)(2,1)} %w_ref.1, bf16[3584,512]{1,0:T(8,128)(2,1)} %v_ref.1), custom_call_target="tpu_custom_call" | custom-call | tf_op jit(solution)/shard_map/gather_all/pallas_call | solution.py:198
  371.3 23.6 %fusion.21 = f32[2048,896]{1,0:T(8,128)} fusion(bf16[2048,4096]{1,0:T(8,128)(2,1)} %get-tuple-element.9, bf16[4096,896]{1,0:T(8,128)(2,1)} %get-tuple-element.12), kind=kOutput, calls=%fused_computation.25 | convolution fusion | flops 15032385536 | bytes 31457280 | tf_op jit(solution)/shard_map/dot_general | solution.py:301
  394.8 25.7 %fusion = f32[2048,64]{0,1:T(8,128)S(1)} fusion(f32[2048,896]{1,0:T(8,128)} %fusion.21, bf16[2048,4096]{1,0:T(8,128)(2,1)} %get-tuple-element.10, bf16[896,4096]{1,0:T(8,128)(2,1)} %get-tuple-element.11, bf16[3584,64]{0,1:T(8,128)(2,1)} %param.15, s32[]{:T(128)S(6)} %select_n.25), kind=kOutput, calls=%fused_computation.1 | convolution fusion | flops 15278276608 | bytes 32096260 | tf_op jit(solution)/shard_map/dot_general | solution.py:310
  420.5 0.0 copy-done
  420.5 0.0 copy-start.1
  420.6 11.0 %fusion.20 = f32[2048,64]{0,1:T(8,128)S(1)} fusion(bf16[2048,4096]{1,0:T(8,128)(2,1)} %get-tuple-element.9, bf16[4096,64]{0,1:T(8,128)(2,1)S(1)} %copy-done), kind=kOutput, calls=%fused_computation.24 | convolution fusion | flops 1073741824 | bytes 17825792 | tf_op jit(solution)/shard_map/dot_general | solution.py:311
  431.5 0.0 copy-start.2
  431.6 0.0 all-reduce.3.cloned.1.call-done
  431.6 0.1 collective-permute-start
  431.6 1.5 collective-permute-start.1
  433.2 1.4 collective-permute-start.2
  434.6 0.6 fusion.3
  435.2 1.0 copy.11
  436.2 0.1 broadcast_in_dim.18
  436.3 1.1 dynamic_update_slice.13
  437.4 0.0 collective-permute-done
  437.4 0.1 copy.12
  437.6 0.7 collective-permute-done.1
  438.2 0.1 copy.13
  438.4 1.1 collective-permute-done.2
  439.5 0.1 copy.14
  439.7 1.1 dynamic_update_slice.14
  440.7 1.1 dynamic_update_slice.15
  441.8 1.1 dynamic_update_slice.16
  442.9 0.4 reshape.20
  443.3 0.0 copy-done.1
  443.3 1.0 fusion.13
  444.3 0.0 copy-done.2
  444.3 1.8 fusion.11
  446.1 0.9 copy.18
  447.1 0.9 convolution_bitcast_fusion
  448.0 0.6 pad.4.part_ref
  448.6 24.2 %sum_over_parts.1 = f32[8,128]{1,0:T(8,128)} custom-call(f32[8,128]{1,0:T(8,128)} %pad.4.part_ref), custom_call_target="tpu_custom_call" | custom-call | tf_op jit(solution)/shard_map/sum_over_parts/pallas_call | solution.py:253
  472.8 1.2 constant_dynamic-slice_fusion
Async XLA Ops:
  6.5 414.0 %copy-start = (bf16[4096,64]{0,1:T(8,128)(2,1)S(1)}, bf16[4096,64]{0,1:T(8,128)(2,1)}, u32[]{:S(2)}) copy-start(bf16[4096,64]{0,1:T(8,128)(2,1)} %param.14) | copy-start | bytes 1572868
  6.5 425.0 %all-reduce.3.cloned.1.call-start = ((), (), s32[]{:S(2)}) async-start(), calls=%async_computation | async-start | bytes 262144 | tf_op jit(solution)/shard_map/psum | solution.py:283
  420.5 22.8 %copy-start.1 = (f32[64,64]{1,0:T(8,128)S(1)}, f32[64,64]{1,0:T(8,128)}, u32[]{:S(2)}) copy-start(f32[64,64]{1,0:T(8,128)} %param.17) | copy-start | bytes 49156
  431.5 12.8 %copy-start.2 = (f32[64,64]{1,0:T(8,128)S(1)}, f32[64,64]{1,0:T(8,128)}, u32[]{:S(2)}) copy-start(f32[64,64]{1,0:T(8,128)} %param.16) | copy-start | bytes 49156
  431.6 5.8 %collective-permute-start = (f32[32,1024]{1,0:T(8,128)}, f32[32,1024]{1,0:T(8,128)S(1)}, u32[]{:S(2)}, u32[]{:S(2)}) collective-permute-start(f32[32,1024]{1,0:T(8,128)} %all-reduce.3.cloned.1.call-done), channel_id=1, source_target_pairs={{0,1},{1,2},{2,3},{3,0},{4,5},{5,6},{6,7},{7,4},{8,9},{9,10},{10,1... | collective-permute-start | bytes 393224 | tf_op jit(solution)/shard_map/ppermute | solution.py:288
  431.6 6.6 %collective-permute-start.1 = (f32[32,1024]{1,0:T(8,128)}, f32[32,1024]{1,0:T(8,128)S(1)}, u32[]{:S(2)}, u32[]{:S(2)}) collective-permute-start(f32[32,1024]{1,0:T(8,128)} %all-reduce.3.cloned.1.call-done), channel_id=1, source_target_pairs={{0,2},{1,3},{2,0},{3,1},{4,6},{5,7},{6,4},{7,5},{8,10},{9,11},{10,... | collective-permute-start | bytes 393224 | tf_op jit(solution)/shard_map/ppermute | solution.py:288
  433.2 6.4 %collective-permute-start.2 = (f32[32,1024]{1,0:T(8,128)}, f32[32,1024]{1,0:T(8,128)S(1)}, u32[]{:S(2)}, u32[]{:S(2)}) collective-permute-start(f32[32,1024]{1,0:T(8,128)} %all-reduce.3.cloned.1.call-done), channel_id=1, source_target_pairs={{0,3},{1,0},{2,1},{3,2},{4,7},{5,4},{6,5},{7,6},{8,11},{9,8},{10,9... | collective-permute-start | bytes 393224 | tf_op jit(solution)/shard_map/ppermute | solution.py:288
Sparse Core Ops, SparseCore 0:
  10.7 112.2 all-reduce.2
